TPU v7x, 32 devices: a whole 2x2x4 slice. The times are simulated.
32 devices in a mesh: gx: 4 (over y, x), gy: 2 (over core), gz: 4 (over z).
Axes of the slice: x: 2, y: 2, z: 4, core: 2. Of those that a mesh axis runs over, the one named last changes fastest.
Arguments:
- inputs: bfloat16 [4, 32, 32, 256], P(None, 'gx', 'gz', 'gy'), may hold values from -6 to 6
- w_in: bfloat16 [16, 4, 3, 3, 3], replicated, may hold values from -0.875 to 0.875
- w_fine_enc: bfloat16 [16, 16, 3, 3, 3], replicated, may hold values from -0.4375 to 0.4375
- w_down_mid: bfloat16 [64, 16, 2, 2, 2], replicated, may hold values from -0.75 to 0.75
- w_mid_enc: bfloat16 [27, 4096], replicated, may hold values from -0.21875 to 0.21875
- w_down_bottom: bfloat16 [8, 16384], replicated, may hold values from -0.375 to 0.375
- w_query: bfloat16 [256, 256], replicated, may hold values from -8 to 8
- w_key: bfloat16 [256, 256], replicated, may hold values from -0.375 to 0.375
- w_value: bfloat16 [256, 256], replicated, may hold values from -0.375 to 0.375
- w_attn_out: bfloat16 [256, 256], replicated, may hold values from -0.375 to 0.375
- w_up_mid: bfloat16 [8, 16384], replicated, may hold values from -0.375 to 0.375
- w_mid_dec: bfloat16 [27, 4096], replicated, may hold values from -0.21875 to 0.21875
- w_up_fine: bfloat16 [64, 16, 2, 2, 2], replicated, may hold values from -0.75 to 0.75
- w_fine_dec: bfloat16 [16, 16, 3, 3, 3], replicated, may hold values from -0.4375 to 0.4375
- w_head: bfloat16 [4, 16], replicated, may hold values from -1.5 to 1.5
Outputs:
- wake: float32 [4, 32, 32, 256], P(None, 'gx', 'gz', 'gy')
All inputs are finite; a program needn't handle non-finite values.
Results may differ from a plain program's by a relative error of at most 0.023.
The roundings to bfloat16 on the way count: a program that leaves them out, or rounds other values in their place, can miss the bound.
Values may be sent and summed in bfloat16 or wider, within the bound.
A program may use at most 64 MiB of HBM per device.

v0:
```python
import functools

import jax
import jax.numpy as jnp
import numpy as np
from jax import lax
from jax.experimental import pallas as pl
from jax.experimental.pallas import tpu as pltpu
from jax.sharding import PartitionSpec as P

BF = jnp.bfloat16
F32 = jnp.float32
MESH = pl.DeviceIdType.MESH
HEADS = 4
DIRS = tuple((dx, dv) for dx in (-1, 0, 1) for dv in (-1, 0, 1) if (dx, dv) != (0, 0))


def constants(nx, nv, ns):
    mv, ms, bv, bs = nv // 2, ns // 2, nv // 4, ns // 4
    g_first = np.zeros((nv + 2, 3, 3, 4, 3, nv + 8, 4), np.float32)
    for k in range(nv + 2):
        for a in range(3):
            for b in range(3):
                for i in range(4):
                    g_first[k, a, b, i, a, k + b + 2, i] = 1
    g_fine = np.zeros((nv, 3, 3, 16, 3, nv + 2, 16), np.float32)
    for k in range(nv):
        for a in range(3):
            for b in range(3):
                for i in range(16):
                    g_fine[k, a, b, i, a, k + b, i] = 1
    g_down = np.zeros((mv, 2, 2, 16, 2, nv, 16), np.float32)
    for k in range(mv):
        for a in range(2):
            for b in range(2):
                for i in range(16):
                    g_down[k, a, b, i, a, 2 * k + b, i] = 1
    g_up = np.zeros((mv, 2, 64, 2, mv, 64), np.float32)
    for k in range(mv):
        for c in range(2):
            for i in range(64):
                g_up[k, c, i, c, k, i] = 1
    lane_down = np.zeros((ns, 2, 2, ms), np.float32)
    for c in range(2):
        for t in range(ms):
            lane_down[2 * t + c, c, :, t] = 1
    cells = 2 * bv * bs
    lane_bottom = np.zeros((2 * bv, ns, 2, 2 * bv, bs), np.float32)
    for q in range(2 * bv):
        for c in range(2):
            for t in range(bs):
                lane_bottom[q, 2 * t + c, c, q, t] = 1
    lane_mid = np.zeros((2 * bv, bs, 2 * bv, 2, 2, ms), np.float32)
    for q in range(2 * bv):
        for c in range(2):
            for t in range(bs):
                lane_mid[q, t, q, c, :, 2 * t + c] = 1
    lane_fine = np.zeros((ns, 2, ns), np.float32)
    for c in range(2):
        for u in range(ms):
            lane_fine[u, c, 2 * u + c] = 1
    arrays = (
        g_first.reshape(nv + 2, 36, 3 * (nv + 8) * 4),
        g_fine.reshape(nv, 144, 3 * (nv + 2) * 16),
        g_down.reshape(mv, 64, 2 * nv * 16),
        g_up.reshape(mv, 128, 2 * mv * 64),
        lane_down.reshape(ns, 2 * ns),
        lane_bottom.reshape(2 * bv, ns, 2 * cells),
        lane_mid.reshape(cells, 2 * bv * 2 * ns),
        lane_fine.reshape(ns, 2 * ns),
    )
    return tuple(jnp.asarray(np.asarray(a, jnp.bfloat16)) for a in arrays)


def dot(a, b):
    return jnp.dot(a, b, preferred_element_type=F32)


def silu(x):
    h = 0.5 * x
    return h + h * jnp.tanh(h)


def rows(ref, x, n):
    part = ref[pl.ds(x, n)]
    return part.reshape(n * part.shape[1], part.shape[2])


def taps(z, m):
    n = z.shape[1]
    return pltpu.roll(z[0:m], 1, 1) + z[m : 2 * m] + pltpu.roll(z[2 * m : 3 * m], n - 1, 1)


def kernel(
    gx, gz, nx, nv, ns,
    inp, w_first, w_enc, w_down, w_menc, w_bot, w_q, w_k, w_v, w_o, w_umid, w_mdec, w_ufine, w_dec, w_hd,
    g_first, g_fine, g_down, g_up, l_down, l_bottom, l_mid, l_fine,
    out,
    p_in, q_in, p_mi, q_mi, p_mu, q_mu, p_fu, q_fu,
    t_first, t_enc, t_dec, t_down, t_up, first, skip, mskip, mdec, bottom, gathered,
    send, recv, csend, crecv, asend, arecv,
):
    mx, mv = nx // 2, nv // 2
    bx, bv = nx // 4, nv // 4
    ix, iy, iz = lax.axis_index("gx"), lax.axis_index("gy"), lax.axis_index("gz")

    def inside(dx, dv):
        ok = None
        for d, i, n in ((dx, ix, gx), (dv, iz, gz)):
            if d:
                here = (i + d >= 0) & (i + d < n)
                ok = here if ok is None else ok & here
        return ok

    def target(dx, dv):
        return (ix + dx, iy, iz + dv)

    for ref in (p_in, p_mi, p_mu, p_fu):
        ref[...] = jnp.zeros_like(ref)

    barrier = pltpu.get_barrier_semaphore()
    pl.semaphore_signal(barrier, inc=1, device_id=(ix, 1 - iy, iz), device_id_type=MESH)
    for d in range(1, gx):
        pl.semaphore_signal(
            barrier, inc=1, device_id=(lax.rem(ix + d, gx), iy, iz), device_id_type=MESH
        )
    count = gx
    for dx, dv in DIRS:
        if dv:
            ok = inside(dx, dv)

            @pl.when(ok)
            def _(dx=dx, dv=dv):
                pl.semaphore_signal(barrier, inc=1, device_id=target(dx, dv), device_id_type=MESH)

            count = count + ok.astype(jnp.int32)
    pl.semaphore_wait(barrier, count)

    def span(d, width, size, unit):
        if d > 0:
            return pl.ds(size * unit, width * unit), pl.ds(0, width * unit)
        if d < 0:
            return pl.ds(width * unit, width * unit), pl.ds((width + size) * unit, width * unit)
        return pl.ds(width * unit, size * unit), pl.ds(width * unit, size * unit)

    def copies(e, p, wx, sx, wv, sv, unit):
        made = []
        for n, (dx, dv) in enumerate(DIRS):
            src_x, dst_x = span(dx, wx, sx, 1)
            src_v, dst_v = span(dv, wv, sv, unit)
            made.append(
                pltpu.make_async_remote_copy(
                    src_ref=p.at[src_x, src_v],
                    dst_ref=p.at[dst_x, dst_v],
                    send_sem=send.at[e, n],
                    recv_sem=recv.at[e, n],
                    device_id=target(dx, dv),
                    device_id_type=MESH,
                )
            )
        return made

    def begin(made):
        for c, (dx, dv) in zip(made, DIRS):
            pl.when(inside(dx, dv))(c.start)

    def finish(e, made, p, q):
        for c, (dx, dv) in zip(made, DIRS):
            pl.when(inside(-dx, -dv))(c.wait_recv)
        across = pltpu.make_async_remote_copy(
            src_ref=p, dst_ref=q, send_sem=csend.at[e], recv_sem=crecv.at[e],
            device_id=(ix, 1 - iy, iz), device_id_type=MESH,
        )
        across.start()
        for c, (dx, dv) in zip(made, DIRS):
            pl.when(inside(dx, dv))(c.wait_send)
        return across

    lane = lax.broadcasted_iota(jnp.int32, (1, ns), 1)

    def edge(width):
        low = jnp.where(iy == 0, 0, ns - width)
        return jnp.where((lane >= low) & (lane < low + width), 1.0, 0.0).astype(BF)

    unit = inp.shape[1] // nv
    p_in[2 : 2 + nx, 4 * unit : (4 + nv) * unit] = inp[...]
    made = copies(0, p_in, 2, nx, 4, nv, unit)
    begin(made)
    for k in range(nv + 2):
        part = dot(w_first[...], g_first[k]).astype(BF)
        for c in range(3):
            t_first[(c * (nv + 2) + k) * 16 : (c * (nv + 2) + k + 1) * 16] = part[c * 16 : c * 16 + 16]
    across = finish(0, made, p_in, q_in)
    for src, dst in ((w_enc, t_enc), (w_dec, t_dec)):
        for k in range(nv):
            part = dot(src[...], g_fine[k]).astype(BF)
            for c in range(3):
                dst[(c * nv + k) * 16 : (c * nv + k + 1) * 16] = part[c * 16 : c * 16 + 16]
    across.wait()

    e2, e1 = edge(2), edge(1)
    fine_rows = (nv + 2) * 16
    row = lax.broadcasted_iota(jnp.int32, (fine_rows, 1), 0)
    v_low = jnp.where(iz > 0, 0, 16)
    v_high = jnp.where(iz < gz - 1, fine_rows, fine_rows - 16)
    v_ok = jnp.where((row >= v_low) & (row < v_high), 1.0, 0.0)
    both = jnp.concatenate([jnp.ones((1, ns), F32), e1.astype(F32)], axis=1)
    keep_first = v_ok * both

    def first_step(x, _):
        field = jnp.concatenate([rows(p_in, x, 3), rows(q_in, x, 3) * e2], axis=1)
        z = taps(dot(t_first[...], field), fine_rows)
        gone = ((x == 0) & (ix == 0)) | ((x == nx + 1) & (ix == gx - 1))
        first[x] = (silu(z) * keep_first * jnp.where(gone, 0.0, 1.0)).astype(BF)
        return 0

    lax.fori_loop(0, nx + 2, first_step, 0)

    def enc_step(x, _):
        z = taps(dot(t_enc[...], rows(first, x, 3)), nv * 16)[:, :ns]
        skip[x] = silu(z).astype(BF)
        return 0

    lax.fori_loop(0, nx, enc_step, 0)

    for k in range(mv):
        part = dot(w_down[...], g_down[k]).astype(BF)
        half = g_down.shape[2]
        for c in range(2):
            t_down[k * 64 : (k + 1) * 64, c * half : (c + 1) * half] = part[c * 64 : (c + 1) * 64]

    def down_step(x, _):
        y = dot(rows(skip, 2 * x, 2), l_down[...]).astype(BF)
        field = jnp.concatenate([y[:, :ns], y[:, ns:]], axis=0)
        p_mi[x + 1, 64 : (mv + 1) * 64] = silu(dot(t_down[...], field)).astype(BF)
        return 0

    lax.fori_loop(0, mx, down_step, 0)

    made = copies(1, p_mi, 1, mx, 1, mv, 64)
    begin(made)
    for k in range(mv):
        part = dot(w_ufine[...], g_up[k]).astype(BF)
        for a in range(2):
            t_up[a * nv * 16 + k * 32 : a * nv * 16 + k * 32 + 32] = part[a * 32 : a * 32 + 32]
    finish(1, made, p_mi, q_mi).wait()

    own_half = jnp.where(lane < ns // 2, 1.0, 0.0).astype(BF)
    mid_edge = jnp.where(lane == jnp.where(iy == 0, ns // 2, ns - 1), 1.0, 0.0).astype(BF)

    def mid_conv(w, p, q, x, v):
        pieces = []
        for a in range(3):
            r = pl.ds(pl.multiple_of(v * 64, 64), 192)
            pieces.append(p[x + a, r] * own_half + q[x + a, r] * mid_edge)
        z = silu(taps(dot(w[...], jnp.concatenate(pieces, axis=0)), 64))
        return jnp.where(lane < ns // 2, z, pltpu.roll(z, ns // 2, 1)).astype(BF)

    def menc_step(n, _):
        x, v = n // mv, n % mv
        mskip[x, pl.ds(pl.multiple_of(v * 64, 64), 64)] = mid_conv(w_menc, p_mi, q_mi, x, v)
        return 0

    lax.fori_loop(0, mx * mv, menc_step, 0)

    halves = []
    for a in range(2):
        total = None
        for n in range(bx * bv):
            x, v = n // bv, n % bv
            term = dot(mskip[2 * x + a, v * 128 : v * 128 + 128], l_bottom[n])
            total = term if total is None else total + term
        halves.append(total.astype(BF))
    field = jnp.concatenate(
        [halves[0][:, :ns], halves[1][:, :ns], halves[0][:, ns:], halves[1][:, ns:]], axis=0
    )
    bottom[...] = silu(dot(w_bot[...], field)).astype(BF)

    peers = []
    for d in range(1, gx):
        c = pltpu.make_async_remote_copy(
            src_ref=bottom, dst_ref=gathered.at[d - 1], send_sem=asend.at[d - 1], recv_sem=arecv.at[d - 1],
            device_id=(lax.rem(ix + d, gx), iy, iz), device_id_type=MESH,
        )
        c.start()
        peers.append(c)

    def normalize(block):
        f = block.astype(F32)
        return (f * lax.rsqrt(jnp.mean(f * f, axis=0, keepdims=True) + 1e-05)).astype(BF)

    chans = bottom.shape[0]
    depth = chans // HEADS
    own = normalize(bottom[...])
    queries = dot(w_q[...], own).astype(BF).astype(F32)
    scores, values = [], []
    for d in range(gx):
        if d:
            peers[d - 1].wait()
            normed = normalize(gathered[d - 1])
        else:
            normed = own
        keys = dot(w_k[...], normed).astype(BF).astype(F32)
        value = dot(w_v[...], normed).astype(BF).astype(F32)
        for turn in range(bx):
            k = pltpu.roll(keys, turn * (ns // bx), 1) if turn else keys
            v = pltpu.roll(value, turn * (ns // bx), 1) if turn else value
            scores.append(
                jnp.sum((queries * k).reshape(HEADS, depth, ns), axis=1, keepdims=True) * (depth**-0.5)
            )
            values.append(v)
    top = functools.reduce(jnp.maximum, scores)
    powers = [jnp.exp(s - top) for s in scores]
    norm = 1.0 / functools.reduce(jnp.add, powers)
    attended = None
    for s, v in zip(powers, values):
        term = (s * norm).astype(BF).astype(F32) * v.reshape(HEADS, depth, ns)
        attended = term if attended is None else attended + term
    attended = attended.reshape(chans, ns).astype(BF)
    mixed = (bottom[...].astype(F32) + dot(w_o[...], attended)).astype(BF)

    spread = dot(mixed, l_mid[...]).astype(BF)
    for n in range(bx * bv):
        x, v = n // bv, n % bv
        field = jnp.concatenate(
            [spread[:, 2 * n * ns : (2 * n + 1) * ns], spread[:, (2 * n + 1) * ns : (2 * n + 2) * ns]], axis=0
        )
        z = dot(w_umid[...], field)
        for a in range(2):
            old = mskip[2 * x + a, v * 128 : v * 128 + 128].astype(F32)
            p_mu[2 * x + a + 1, 64 + v * 128 : 64 + v * 128 + 128] = (z[a * 128 : a * 128 + 128] + old).astype(BF)

    made = copies(2, p_mu, 1, mx, 1, mv, 64)
    begin(made)
    finish(2, made, p_mu, q_mu).wait()

    def mdec_step(n, _):
        x, v = n // mv, n % mv
        mdec[x, pl.ds(pl.multiple_of(v * 64, 64), 64)] = mid_conv(w_mdec, p_mu, q_mu, x, v)
        return 0

    lax.fori_loop(0, mx * mv, mdec_step, 0)

    def up_step(x, _):
        y = dot(mdec[x], l_fine[...]).astype(BF)
        field = jnp.concatenate([y[:, :ns], y[:, ns:]], axis=0)
        z = dot(t_up[...], field)
        m = nv * 16
        for a in range(2):
            old = skip[2 * x + a].astype(F32)
            p_fu[2 * x + a + 1, 16 : 16 + m] = (z[a * m : (a + 1) * m] + old).astype(BF)
        return 0

    lax.fori_loop(0, mx, up_step, 0)

    made = copies(3, p_fu, 1, nx, 1, nv, 16)
    begin(made)
    finish(3, made, p_fu, q_fu).wait()

    def dec_step(x, _):
        field = jnp.concatenate([rows(p_fu, x, 3), rows(q_fu, x, 3) * e1], axis=1)
        z = taps(dot(t_dec[...], field), nv * 16)[:, :ns]
        wake = dot(w_hd[...], silu(z).astype(BF))
        for o in range(4):
            out[o, x] = wake[o * nv : (o + 1) * nv]
        return 0

    lax.fori_loop(0, nx, dec_step, 0)


def on_device(
    gx, gz, inputs, w_in, w_fine_enc, w_down_mid, w_mid_enc, w_down_bottom, w_query, w_key, w_value,
    w_attn_out, w_up_mid, w_mid_dec, w_up_fine, w_fine_dec, w_head,
):
    _, nx, nv, ns = inputs.shape
    mx, mv = nx // 2, nv // 2
    cells = (nx // 4) * (nv // 4) * (ns // 4)
    assert cells == ns and 2 * (nx // 4) == mx

    def taps_out(w):
        o, i = w.shape[:2]
        return w.transpose(4, 0, 2, 3, 1).reshape(w.shape[4] * o, -1)

    def mid(w):
        return w.reshape(3, 3, 3, 64, 64).transpose(2, 3, 0, 1, 4).reshape(192, 576)

    local = inputs.transpose(1, 2, 0, 3).reshape(nx, nv * 4, ns)
    w_bot = w_down_bottom.reshape(2, 2, 2, 256, 64).transpose(3, 2, 0, 1, 4).reshape(256, 512)
    w_umid = w_up_mid.reshape(2, 2, 2, 256, 64).transpose(0, 1, 4, 2, 3).reshape(256, 512)
    w_ufine = w_up_fine.transpose(2, 3, 1, 4, 0).reshape(64, 128)
    w_hd = (w_head[:, None, None, :] * jnp.eye(nv, dtype=BF)[None, :, :, None]).reshape(4 * nv, nv * 16)
    operands = (
        local, taps_out(w_in), taps_out(w_fine_enc), taps_out(w_down_mid), mid(w_mid_enc), w_bot,
        w_query, w_key, w_value, w_attn_out, w_umid, mid(w_mid_dec), w_ufine, taps_out(w_fine_dec), w_hd,
    ) + constants(nx, nv, ns)
    vm = pltpu.VMEM
    shapes = []
    for shape in (
        (nx + 4, (nv + 8) * 4, ns), (mx + 2, (mv + 2) * 64, ns), (mx + 2, (mv + 2) * 64, ns),
        (nx + 2, (nv + 2) * 16, ns),
    ):
        shapes += [vm(shape, BF), vm(shape, BF)]
    return pl.pallas_call(
        functools.partial(kernel, gx, gz, nx, nv, ns),
        out_shape=jax.ShapeDtypeStruct(inputs.shape, F32),
        in_specs=[pl.BlockSpec(memory_space=pltpu.VMEM)] * len(operands),
        out_specs=pl.BlockSpec(memory_space=pltpu.VMEM),
        scratch_shapes=shapes + [
            vm((3 * (nv + 2) * 16, 3 * (nv + 8) * 4), BF),
            vm((3 * nv * 16, 3 * (nv + 2) * 16), BF),
            vm((3 * nv * 16, 3 * (nv + 2) * 16), BF),
            vm((mv * 64, 4 * nv * 16), BF),
            vm((2 * nv * 16, 2 * mv * 64), BF),
            vm((nx + 2, (nv + 2) * 16, 2 * ns), BF),
            vm((nx, nv * 16, ns), BF),
            vm((mx, mv * 64, ns), BF),
            vm((mx, mv * 64, ns), BF),
            vm((256, cells), BF),
            vm((max(gx - 1, 1), 256, cells), BF),
            pltpu.SemaphoreType.DMA((4, 8)),
            pltpu.SemaphoreType.DMA((4, 8)),
            pltpu.SemaphoreType.DMA((4,)),
            pltpu.SemaphoreType.DMA((4,)),
            pltpu.SemaphoreType.DMA((max(gx - 1, 1),)),
            pltpu.SemaphoreType.DMA((max(gx - 1, 1),)),
        ],
        compiler_params=pltpu.CompilerParams(
            collective_id=0, has_side_effects=True, vmem_limit_bytes=48 * 1024 * 1024
        ),
    )(*operands)


def solution(mesh):
    cells = P(None, "gx", "gz", "gy")
    return jax.shard_map(
        functools.partial(on_device, mesh.shape["gx"], mesh.shape["gz"]),
        mesh=mesh, in_specs=(cells,) + (P(),) * 14, out_specs=cells, check_vma=False,
    )
```

profile of v0, /device:TPU:3, one launch (start us, length us, event | category | flops | bytes accessed | tf_op | source)
XLA Modules:
  0.0 95.9 jit_solution(5528943847271779041)
XLA Ops:
  0.0 1.5 %reshape.59 = bf16[3,3,3,64,64]{4,3,2,1,0:T(8,128)(2,1)S(1)} reshape(bf16[27,4096]{1,0:T(8,128)(2,1)} %param.27) | data formatting | bytes 442368 | tf_op jit(solution)/shard_map/reshape | solution.py:385
  1.9 0.4 reshape.60.w_menc
  2.3 0.4 reshape.65
  3.1 0.4 reshape.66.w_mdec
  3.5 0.5 reshape.63
  4.5 0.5 reshape.61
  5.0 0.9 copy.39
  6.0 1.2 %copy.46.w_bot = bf16[256,512]{1,0:T(8,128)(2,1)S(1)} copy(bf16[256,512]{0,1:T(8,128)(2,1)} %bitcast.32) | data formatting | bytes 524288 | tf_op jit(solution)/shard_map/reshape | solution.py:388
  7.2 1.6 %copy.36 = bf16[3,16,3,3,16]{4,3,2,1,0:T(4,128)(2,1)} copy(bf16[3,16,3,3,16]{4,1,0,3,2:T(8,128)(2,1)} %bitcast.33) | data formatting | bytes 27648 | tf_op jit(solution)/shard_map/transpose | solution.py:382
  8.8 1.7 %reshape.57.w_enc = bf16[48,144]{1,0:T(8,128)(2,1)} reshape(bf16[3,16,3,3,16]{4,3,2,1,0:T(4,128)(2,1)} %copy.36) | data formatting | bytes 27648 | tf_op jit(solution)/shard_map/reshape | solution.py:382
  10.5 1.6 %copy.43 = bf16[3,16,3,3,16]{4,3,2,1,0:T(4,128)(2,1)} copy(bf16[3,16,3,3,16]{4,1,0,3,2:T(8,128)(2,1)} %bitcast.34) | data formatting | bytes 27648 | tf_op jit(solution)/shard_map/transpose | solution.py:382
  12.1 1.7 %reshape.68.w_dec = bf16[48,144]{1,0:T(8,128)(2,1)} reshape(bf16[3,16,3,3,16]{4,3,2,1,0:T(4,128)(2,1)} %copy.43) | data formatting | bytes 27648 | tf_op jit(solution)/shard_map/reshape | solution.py:382
  14.0 0.8 broadcast_multiply_fusion
  14.8 0.9 copy.34
  15.7 1.4 %copy.35 = bf16[3,16,3,3,4]{1,0,4,3,2:T(4,128)(2,1)} copy(bf16[3,16,3,3,4]{1,4,0,3,2:T(4,128)(2,1)} %bitcast.38) | data formatting | bytes 6912 | tf_op jit(solution)/shard_map/transpose | solution.py:382
  17.1 1.5 %reshape.56 = bf16[48,36]{0,1:T(8,128)(2,1)} reshape(bf16[3,16,3,3,4]{1,0,4,3,2:T(4,128)(2,1)} %copy.35) | data formatting | bytes 6912 | tf_op jit(solution)/shard_map/reshape | solution.py:382
  18.6 1.4 %copy.44.w_first = bf16[48,36]{1,0:T(8,128)(2,1)} copy(bf16[48,36]{0,1:T(8,128)(2,1)} %reshape.56) | data formatting | bytes 6912 | tf_op jit(solution)/shard_map/reshape | solution.py:382
  20.0 1.4 %copy.42 = bf16[2,2,16,2,64]{4,3,2,1,0:T(2,128)(2,1)} copy(bf16[2,2,16,2,64]{4,3,1,0,2:T(2,128)(2,1)} %bitcast.37) | data formatting | bytes 32768 | tf_op jit(solution)/shard_map/transpose | solution.py:390
  21.4 1.4 %reshape.67.w_ufine = bf16[64,128]{1,0:T(8,128)(2,1)} reshape(bf16[2,2,16,2,64]{4,3,2,1,0:T(2,128)(2,1)} %copy.42) | data formatting | bytes 32768 | tf_op jit(solution)/shard_map/reshape | solution.py:390
  22.8 0.9 copy-done.5
  23.7 0.9 copy-done.6
  24.6 0.9 copy-done.7
  25.6 0.9 copy-done.8
  26.5 0.9 copy-done.9
  27.4 0.7 copy-done.10
  28.1 0.7 copy-done.11
  28.8 0.8 copy-done.12
  29.7 0.8 copy-done.13
  30.5 0.7 copy-done.14
  31.2 0.7 copy-done.15
  31.9 63.3 %shard_map.217 = f32[4,8,8,128]{3,2,1,0:T(8,128)S(1)} custom-call(bf16[8,32,128]{2,1,0:T(8,128)(2,1)S(1)} %bitcast.26, bf16[48,36]{1,0:T(8,128)(2,1)S(1)} %copy-done.15, bf16[48,144]{1,0:T(8,128)(2,1)S(1)} %copy-done.10, bf16[128,64]{1,0:T(8,128)(2,1)S(1)} %copy.45.w_down, bf16[192,576]{1,0:T(8,128)(2,1)S(1)} %reshape.60.w_menc, ...), custom_call_target="tpu_custom_call" | custom-call | tf_op jit(solution)/shard_map/pallas_call | solution.py:403
  95.2 0.7 copy.53
  (38 shorter events, 1.6 us)
Async XLA Ops:
  0.0 2.3 %copy-start.18 = (bf16[27,4096]{1,0:T(8,128)(2,1)S(1)}, bf16[27,4096]{1,0:T(8,128)(2,1)}, u32[]{:S(2)}) copy-start(bf16[27,4096]{1,0:T(8,128)(2,1)} %param.34) | copy-start | bytes 663556
  2.3 1.3 %copy-start.16 = (bf16[8,16384]{1,0:T(8,128)(2,1)S(1)}, bf16[8,16384]{1,0:T(8,128)(2,1)}, u32[]{:S(2)}) copy-start(bf16[8,16384]{1,0:T(8,128)(2,1)} %param.33) | copy-start | bytes 786436
  3.5 1.0 copy-start.17
  5.0 8.7 %copy-start.19 = (bf16[64,16,2,2,2]{0,4,3,2,1:T(2,128)(2,1)S(1)}, bf16[64,16,2,2,2]{0,4,3,2,1:T(2,128)(2,1)}, u32[]{:S(2)}) copy-start(bf16[64,16,2,2,2]{0,4,3,2,1:T(2,128)(2,1)} %param.26) | copy-start | bytes 49156
  5.0 17.8 %copy-start.3 = (bf16[128,1024]{1,0:T(8,128)(2,1)S(1)}, bf16[128,1024]{1,0:T(8,128)(2,1)}, u32[]{:S(2)}) copy-start(bf16[128,1024]{1,0:T(8,128)(2,1)} %constant.22.clone.l_mid) | copy-start | bytes 786436
  5.0 17.8 %copy-start.4 = (bf16[10,36,192]{2,1,0:T(8,128)(2,1)S(1)}, bf16[10,36,192]{2,1,0:T(8,128)(2,1)}, u32[]{:S(2)}) copy-start(bf16[10,36,192]{2,1,0:T(8,128)(2,1)} %constant.16.clone.g_first) | copy-start | bytes 414724
  5.9 16.9 %copy-start = (bf16[8,144,480]{2,1,0:T(8,128)(2,1)S(1)}, bf16[8,144,480]{2,1,0:T(8,128)(2,1)}, u32[]{:S(2)}) copy-start(bf16[8,144,480]{2,1,0:T(8,128)(2,1)} %constant.17.clone.g_fine) | copy-start | bytes 3317764
  5.9 16.9 %copy-start.1 = (bf16[4,128,512]{2,1,0:T(8,128)(2,1)S(1)}, bf16[4,128,512]{2,1,0:T(8,128)(2,1)}, u32[]{:S(2)}) copy-start(bf16[4,128,512]{2,1,0:T(8,128)(2,1)} %constant.19.clone.g_up) | copy-start | bytes 1572868
  6.0 16.9 %copy-start.2 = (bf16[4,128,256]{2,1,0:T(8,128)(2,1)S(1)}, bf16[4,128,256]{2,1,0:T(8,128)(2,1)}, u32[]{:S(2)}) copy-start(bf16[4,128,256]{2,1,0:T(8,128)(2,1)} %constant.21.clone.l_bottom) | copy-start | bytes 786436
  22.8 0.9 copy-start.5
  23.7 0.9 copy-start.6
  24.6 0.9 copy-start.7
  25.6 0.9 copy-start.8
  26.5 0.9 copy-start.9
  27.4 0.7 copy-start.10
  28.1 0.7 copy-start.11
  28.8 0.8 copy-start.12
  29.7 0.8 copy-start.13
  30.5 0.7 copy-start.14
  31.2 0.7 copy-start.15
where the time goes:
time: 96.9 us; the launch traced here: 95.9 us
  Pallas kernels  63.3 us (65%)
  local copies, waits for them, and re-layouts  31.6 us (33%)
    pallas_call x1, Pallas kernels, on_device(): pl.pallas_call(functools.partial(kernel, gx, gz, nx, nv, ns), out_shape=j...  63.3 us
    unnamed x42, local copies, waits for them, and re-layouts  9.93 us
    reshape x6, local copies, waits for them, and re-layouts, taps_out(): return w.transpose(4, 0, 2, 3, 1).reshape(w.shape[4] * o, -1)  6.36 us
    transpose x4, local copies, waits for them, and re-layouts, taps_out(): return w.transpose(4, 0, 2, 3, 1).reshape(w.shape[4] * o, -1)  4.62 us
    reshape x6, local copies, waits for them, and re-layouts, mid(): return w.reshape(3, 3, 3, 64, 64).transpose(2, 3, 0, 1, 4).reshape(192, 576)  3.45 us

commit v1 on v0

--- a/solution.py
+++ b/solution.py
@@ -86,6 +86,13 @@
     return part.reshape(n * part.shape[1], part.shape[2])
 
 
+def by_tap(ref):
+    parts = []
+    for c in range(3):
+        parts.append(jnp.concatenate([ref[ab * 3 + c].astype(F32) for ab in range(9)], axis=1))
+    return jnp.concatenate(parts, axis=0).astype(BF)
+
+
 def taps(z, m):
     n = z.shape[1]
     return pltpu.roll(z[0:m], 1, 1) + z[m : 2 * m] + pltpu.roll(z[2 * m : 3 * m], n - 1, 1)
@@ -186,14 +193,16 @@
     p_in[2 : 2 + nx, 4 * unit : (4 + nv) * unit] = inp[...]
     made = copies(0, p_in, 2, nx, 4, nv, unit)
     begin(made)
+    flat = by_tap(w_first)
     for k in range(nv + 2):
-        part = dot(w_first[...], g_first[k]).astype(BF)
+        part = dot(flat, g_first[k]).astype(BF)
         for c in range(3):
             t_first[(c * (nv + 2) + k) * 16 : (c * (nv + 2) + k + 1) * 16] = part[c * 16 : c * 16 + 16]
     across = finish(0, made, p_in, q_in)
     for src, dst in ((w_enc, t_enc), (w_dec, t_dec)):
+        flat = by_tap(src)
         for k in range(nv):
-            part = dot(src[...], g_fine[k]).astype(BF)
+            part = dot(flat, g_fine[k]).astype(BF)
             for c in range(3):
                 dst[(c * nv + k) * 16 : (c * nv + k + 1) * 16] = part[c * 16 : c * 16 + 16]
     across.wait()
@@ -381,6 +390,9 @@
         o, i = w.shape[:2]
         return w.transpose(4, 0, 2, 3, 1).reshape(w.shape[4] * o, -1)
 
+    def each_tap(w):
+        return w.transpose(2, 3, 4, 0, 1).reshape(27, w.shape[0], w.shape[1])
+
     def mid(w):
         return w.reshape(3, 3, 3, 64, 64).transpose(2, 3, 0, 1, 4).reshape(192, 576)
 
@@ -390,8 +402,8 @@
     w_ufine = w_up_fine.transpose(2, 3, 1, 4, 0).reshape(64, 128)
     w_hd = (w_head[:, None, None, :] * jnp.eye(nv, dtype=BF)[None, :, :, None]).reshape(4 * nv, nv * 16)
     operands = (
-        local, taps_out(w_in), taps_out(w_fine_enc), taps_out(w_down_mid), mid(w_mid_enc), w_bot,
-        w_query, w_key, w_value, w_attn_out, w_umid, mid(w_mid_dec), w_ufine, taps_out(w_fine_dec), w_hd,
+        local, each_tap(w_in), each_tap(w_fine_enc), taps_out(w_down_mid), mid(w_mid_enc), w_bot,
+        w_query, w_key, w_value, w_attn_out, w_umid, mid(w_mid_dec), w_ufine, each_tap(w_fine_dec), w_hd,
     ) + constants(nx, nv, ns)
     vm = pltpu.VMEM
     shapes = []

time: 96.9 us -> 85.7 us (0.88)
  local copies, waits for them, and re-layouts: 31.6 us -> 21.4 us
    reshape x6 -> x2, local copies, waits for them, and re-layouts: 6.36 us -> 0.21 us  [taps_out(): return w.transpose(4, 0, 2, 3, 1).reshape(w.shape[4] * o, -1)]
    transpose x4 -> x1, local copies, waits for them, and re-layouts: 4.62 us -> 0.02 us  [taps_out(): return w.transpose(4, 0, 2, 3, 1).reshape(w.shape[4] * o, -1)]
    transpose x1, local copies, waits for them, and re-layouts: 0.9 us -> 2.07 us  [on_device(): w_down_bottom.reshape(2, 2, 2, 256, 64).transpose(3, 2, 0, 1, 4)]
    unnamed x42, local copies, waits for them, and re-layouts: 9.93 us -> 8.9 us
where the time goes in v1:
time: 85.7 us; the launch traced here: 85.1 us
  Pallas kernels  63.5 us (74%)
  local copies, waits for them, and re-layouts  21.4 us (25%)
    pallas_call x1, Pallas kernels, on_device(): pl.pallas_call(functools.partial(kernel, gx, gz, nx, nv, ns), out_shape=j...  63.5 us
    unnamed x42, local copies, waits for them, and re-layouts  8.9 us
    reshape x6, local copies, waits for them, and re-layouts, mid(): return w.reshape(3, 3, 3, 64, 64).transpose(2, 3, 0, 1, 4).reshape(192, 576)  3.45 us
    reshape x2, local copies, waits for them, and re-layouts, on_device(): w_down_bottom.reshape(2, 2, 2, 256, 64).transpose(3, 2, 0, 1, 4)  2.43 us
    transpose x1, local copies, waits for them, and re-layouts, on_device(): w_down_bottom.reshape(2, 2, 2, 256, 64).transpose(3, 2, 0, 1, 4)  2.07 us

profile of v1, /device:TPU:3, one launch (start us, length us, event | category | flops | bytes accessed | tf_op | source)
XLA Modules:
  0.0 85.1 jit_solution(8227118623309824442)
XLA Ops:
  0.0 1.5 %reshape.59 = bf16[3,3,3,64,64]{4,3,2,1,0:T(8,128)(2,1)S(1)} reshape(bf16[27,4096]{1,0:T(8,128)(2,1)} %param.27) | data formatting | bytes 442368 | tf_op jit(solution)/shard_map/reshape | solution.py:397
  1.5 0.4 copy.46
  1.9 0.4 reshape.60.w_menc
  2.3 0.4 reshape.65
  2.7 0.4 copy.45
  3.1 0.4 reshape.66.w_mdec
  3.5 0.5 reshape.63
  4.1 0.2 copy.37
  4.4 0.1 copy-done.15
  4.5 1.3 %reshape.61 = bf16[2,2,2,256,64]{4,3,2,1,0:T(8,128)(2,1)} reshape(bf16[8,16384]{1,0:T(8,128)(2,1)S(1)} %copy-done.15) | data formatting | bytes 524288 | tf_op jit(solution)/shard_map/reshape | solution.py:400
  5.8 2.1 %copy.36 = bf16[256,2,2,2,64]{0,4,3,2,1:T(8,128)(2,1)} copy(bf16[256,2,2,2,64]{4,0,1,3,2:T(8,128)(2,1)} %bitcast.36) | data formatting | bytes 524288 | tf_op jit(solution)/shard_map/transpose | solution.py:400
  7.9 1.1 %copy.41.w_bot = bf16[256,512]{1,0:T(8,128)(2,1)S(1)} copy(bf16[256,512]{0,1:T(8,128)(2,1)} %bitcast.38) | data formatting | bytes 524288 | tf_op jit(solution)/shard_map/reshape | solution.py:400
  9.0 0.3 copy.33
  9.3 0.1 reshape.58
  9.4 0.1 copy.40.w_down
  9.5 0.1 broadcast_multiply_fusion
  9.6 0.1 mul.20.w_hd
  9.7 0.9 %copy.32 = bf16[8,8,4,128]{3,2,1,0:T(4,128)(2,1)S(1)} copy(bf16[8,8,4,128]{3,1,0,2:T(8,128)(2,1)} %bitcast.39) | data formatting | bytes 131072 | tf_op jit(solution)/shard_map/transpose | solution.py:399
  10.6 1.4 %copy.39 = bf16[2,2,16,2,64]{4,3,2,1,0:T(2,128)(2,1)} copy(bf16[2,2,16,2,64]{4,3,1,0,2:T(2,128)(2,1)} %bitcast.41) | data formatting | bytes 32768 | tf_op jit(solution)/shard_map/transpose | solution.py:402
  12.0 0.8 reshape.67.w_ufine
  12.9 0.0 copy-start.4
  12.9 0.9 %copy-done.4 = bf16[10,36,192]{2,1,0:T(8,128)(2,1)S(1)} copy-done((bf16[10,36,192]{2,1,0:T(8,128)(2,1)S(1)}, bf16[10,36,192]{2,1,0:T(8,128)(2,1)}, u32[]{:S(2)}) %copy-start.4) | copy-done | bytes 138264
  13.9 0.9 %copy-done.5 = bf16[256,256]{1,0:T(8,128)(2,1)S(1)} copy-done((bf16[256,256]{1,0:T(8,128)(2,1)S(1)}, bf16[256,256]{1,0:T(8,128)(2,1)}, u32[]{:S(2)}) %copy-start.5) | copy-done | bytes 131096
  14.8 0.9 %copy-done.6 = bf16[256,256]{1,0:T(8,128)(2,1)S(1)} copy-done((bf16[256,256]{1,0:T(8,128)(2,1)S(1)}, bf16[256,256]{1,0:T(8,128)(2,1)}, u32[]{:S(2)}) %copy-start.6) | copy-done | bytes 131096
  15.7 0.9 %copy-done.7 = bf16[256,256]{1,0:T(8,128)(2,1)S(1)} copy-done((bf16[256,256]{1,0:T(8,128)(2,1)S(1)}, bf16[256,256]{1,0:T(8,128)(2,1)}, u32[]{:S(2)}) %copy-start.7) | copy-done | bytes 131096
  16.6 0.9 %copy-done.8 = bf16[256,256]{1,0:T(8,128)(2,1)S(1)} copy-done((bf16[256,256]{1,0:T(8,128)(2,1)S(1)}, bf16[256,256]{1,0:T(8,128)(2,1)}, u32[]{:S(2)}) %copy-start.8) | copy-done | bytes 131096
  17.5 0.9 %copy-done.9 = bf16[4,64,256]{2,1,0:T(8,128)(2,1)S(1)} copy-done((bf16[4,64,256]{2,1,0:T(8,128)(2,1)S(1)}, bf16[4,64,256]{2,1,0:T(8,128)(2,1)}, u32[]{:S(2)}) %copy-start.9) | copy-done | bytes 131096
  18.4 0.9 %copy-done.10 = bf16[16,16,3,3,3]{1,0,4,3,2:T(8,128)(2,1)S(1)} copy-done((bf16[16,16,3,3,3]{1,0,4,3,2:T(8,128)(2,1)S(1)}, bf16[16,16,3,3,3]{1,0,4,3,2:T(8,128)(2,1)}, u32[]{:S(2)}) %copy-start.10) | copy-done | bytes 13848
  19.3 0.9 %copy-done.11 = bf16[16,16,3,3,3]{1,0,4,3,2:T(8,128)(2,1)S(1)} copy-done((bf16[16,16,3,3,3]{1,0,4,3,2:T(8,128)(2,1)S(1)}, bf16[16,16,3,3,3]{1,0,4,3,2:T(8,128)(2,1)}, u32[]{:S(2)}) %copy-start.11) | copy-done | bytes 13848
  20.2 0.8 copy-done.13
  21.0 63.5 %shard_map.217 = f32[4,8,8,128]{3,2,1,0:T(8,128)S(1)} custom-call(bf16[8,32,128]{2,1,0:T(8,128)(2,1)S(1)} %bitcast.30, bf16[27,16,4]{2,1,0:T(8,128)(2,1)S(1)} %bitcast.29, bf16[27,16,16]{2,1,0:T(8,128)(2,1)S(1)} %bitcast.31, bf16[128,64]{1,0:T(8,128)(2,1)S(1)} %copy.40.w_down, bf16[192,576]{1,0:T(8,128)(2,1)S(1)} %reshape.60.w_menc, ...), custom_call_target="tpu_custom_call" | custom-call | tf_op jit(solution)/shard_map/pallas_call | solution.py:415
  84.5 0.7 copy.48
  (32 shorter events, 0.1 us)
Async XLA Ops:
  0.0 2.3 %copy-start.16 = (bf16[27,4096]{1,0:T(8,128)(2,1)S(1)}, bf16[27,4096]{1,0:T(8,128)(2,1)}, u32[]{:S(2)}) copy-start(bf16[27,4096]{1,0:T(8,128)(2,1)} %param.34) | copy-start | bytes 663556
  2.3 1.3 %copy-start.14 = (bf16[8,16384]{1,0:T(8,128)(2,1)S(1)}, bf16[8,16384]{1,0:T(8,128)(2,1)}, u32[]{:S(2)}) copy-start(bf16[8,16384]{1,0:T(8,128)(2,1)} %param.33) | copy-start | bytes 786436
  3.5 1.0 %copy-start.15 = (bf16[8,16384]{1,0:T(8,128)(2,1)S(1)}, bf16[8,16384]{1,0:T(8,128)(2,1)}, u32[]{:S(2)}) copy-start(bf16[8,16384]{1,0:T(8,128)(2,1)} %param.28) | copy-start | bytes 786436
  4.4 4.6 %copy-start.18 = (bf16[16,4,3,3,3]{0,1,4,3,2:T(4,128)(2,1)S(1)}, bf16[16,4,3,3,3]{0,1,4,3,2:T(4,128)(2,1)}, u32[]{:S(2)}) copy-start(bf16[16,4,3,3,3]{0,1,4,3,2:T(4,128)(2,1)} %param.24) | copy-start | bytes 10372
  4.4 4.9 %copy-start.17 = (bf16[64,16,2,2,2]{0,4,3,2,1:T(2,128)(2,1)S(1)}, bf16[64,16,2,2,2]{0,4,3,2,1:T(2,128)(2,1)}, u32[]{:S(2)}) copy-start(bf16[64,16,2,2,2]{0,4,3,2,1:T(2,128)(2,1)} %param.26) | copy-start | bytes 49156
  4.5 5.0 %copy-start.19 = (bf16[4,16]{1,0:T(4,128)(2,1)S(1)}, bf16[4,16]{1,0:T(4,128)(2,1)}, u32[]{:S(2)}) copy-start(bf16[4,16]{1,0:T(4,128)(2,1)} %param.37) | copy-start | bytes 388
  4.5 8.4 %copy-start.3 = (bf16[128,1024]{1,0:T(8,128)(2,1)S(1)}, bf16[128,1024]{1,0:T(8,128)(2,1)}, u32[]{:S(2)}) copy-start(bf16[128,1024]{1,0:T(8,128)(2,1)} %constant.22.clone.l_mid) | copy-start | bytes 786436
  4.5 8.4 %copy-start.12 = (bf16[128,256]{1,0:T(8,128)(2,1)S(1)}, bf16[128,256]{1,0:T(8,128)(2,1)}, u32[]{:S(2)}) copy-start(bf16[128,256]{1,0:T(8,128)(2,1)} %constant.20.clone.l_down) | copy-start | bytes 196612
  5.8 7.1 %copy-start = (bf16[8,144,480]{2,1,0:T(8,128)(2,1)S(1)}, bf16[8,144,480]{2,1,0:T(8,128)(2,1)}, u32[]{:S(2)}) copy-start(bf16[8,144,480]{2,1,0:T(8,128)(2,1)} %constant.17.clone.g_fine) | copy-start | bytes 3317764
  5.8 7.1 %copy-start.1 = (bf16[4,128,512]{2,1,0:T(8,128)(2,1)S(1)}, bf16[4,128,512]{2,1,0:T(8,128)(2,1)}, u32[]{:S(2)}) copy-start(bf16[4,128,512]{2,1,0:T(8,128)(2,1)} %constant.19.clone.g_up) | copy-start | bytes 1572868
  5.8 7.1 %copy-start.2 = (bf16[4,128,256]{2,1,0:T(8,128)(2,1)S(1)}, bf16[4,128,256]{2,1,0:T(8,128)(2,1)}, u32[]{:S(2)}) copy-start(bf16[4,128,256]{2,1,0:T(8,128)(2,1)} %constant.21.clone.l_bottom) | copy-start | bytes 786436
  12.9 0.9 %copy-start.4 = (bf16[10,36,192]{2,1,0:T(8,128)(2,1)S(1)}, bf16[10,36,192]{2,1,0:T(8,128)(2,1)}, u32[]{:S(2)}) copy-start(bf16[10,36,192]{2,1,0:T(8,128)(2,1)} %constant.16.clone.g_first) | copy-start | bytes 414724
  13.9 0.9 %copy-start.5 = (bf16[256,256]{1,0:T(8,128)(2,1)S(1)}, bf16[256,256]{1,0:T(8,128)(2,1)}, u32[]{:S(2)}) copy-start(bf16[256,256]{1,0:T(8,128)(2,1)} %w_q.1) | copy-start | bytes 393220
  14.8 0.9 %copy-start.6 = (bf16[256,256]{1,0:T(8,128)(2,1)S(1)}, bf16[256,256]{1,0:T(8,128)(2,1)}, u32[]{:S(2)}) copy-start(bf16[256,256]{1,0:T(8,128)(2,1)} %w_k.1) | copy-start | bytes 393220
  15.7 0.9 %copy-start.7 = (bf16[256,256]{1,0:T(8,128)(2,1)S(1)}, bf16[256,256]{1,0:T(8,128)(2,1)}, u32[]{:S(2)}) copy-start(bf16[256,256]{1,0:T(8,128)(2,1)} %w_v.1) | copy-start | bytes 393220
  16.6 0.9 %copy-start.8 = (bf16[256,256]{1,0:T(8,128)(2,1)S(1)}, bf16[256,256]{1,0:T(8,128)(2,1)}, u32[]{:S(2)}) copy-start(bf16[256,256]{1,0:T(8,128)(2,1)} %w_o.1) | copy-start | bytes 393220
  17.5 0.9 %copy-start.9 = (bf16[4,64,256]{2,1,0:T(8,128)(2,1)S(1)}, bf16[4,64,256]{2,1,0:T(8,128)(2,1)}, u32[]{:S(2)}) copy-start(bf16[4,64,256]{2,1,0:T(8,128)(2,1)} %constant.18.clone.g_down) | copy-start | bytes 393220
  18.4 0.9 %copy-start.10 = (bf16[16,16,3,3,3]{1,0,4,3,2:T(8,128)(2,1)S(1)}, bf16[16,16,3,3,3]{1,0,4,3,2:T(8,128)(2,1)}, u32[]{:S(2)}) copy-start(bf16[16,16,3,3,3]{1,0,4,3,2:T(8,128)(2,1)} %param.25) | copy-start | bytes 41476
  19.3 0.9 %copy-start.11 = (bf16[16,16,3,3,3]{1,0,4,3,2:T(8,128)(2,1)S(1)}, bf16[16,16,3,3,3]{1,0,4,3,2:T(8,128)(2,1)}, u32[]{:S(2)}) copy-start(bf16[16,16,3,3,3]{1,0,4,3,2:T(8,128)(2,1)} %param.36) | copy-start | bytes 41476
  20.2 0.8 copy-start.13

commit v2 on v1

--- a/solution.py
+++ b/solution.py
@@ -12,6 +12,7 @@
 F32 = jnp.float32
 MESH = pl.DeviceIdType.MESH
 HEADS = 4
+FAR = 17
 DIRS = tuple((dx, dv) for dx in (-1, 0, 1) for dv in (-1, 0, 1) if (dx, dv) != (0, 0))
 
 
@@ -100,13 +101,24 @@
 
 def kernel(
     gx, gz, nx, nv, ns,
-    inp, w_first, w_enc, w_down, w_menc, w_bot, w_q, w_k, w_v, w_o, w_umid, w_mdec, w_ufine, w_dec, w_hd,
-    g_first, g_fine, g_down, g_up, l_down, l_bottom, l_mid, l_fine,
-    out,
-    p_in, q_in, p_mi, q_mi, p_mu, q_mu, p_fu, q_fu,
-    t_first, t_enc, t_dec, t_down, t_up, first, skip, mskip, mdec, bottom, gathered,
-    send, recv, csend, crecv, asend, arecv,
+    inp, w_first, w_enc, w_down, g_first, w_dec, *rest
 ):
+    far, rest = rest[:FAR], rest[FAR:]
+    (
+        out,
+        p_in, q_in, p_mi, q_mi, p_mu, q_mu, p_fu, q_fu,
+        t_first, t_enc, t_dec, t_down, t_up, first, skip, mskip, mdec, bottom, gathered,
+        send, recv, csend, crecv, asend, arecv, fsem,
+    ), near = rest[:-FAR], rest[-FAR:]
+    fetches = []
+    for n in range(FAR):
+        c = pltpu.make_async_copy(far[n], near[n], fsem.at[n])
+        c.start()
+        fetches.append(c)
+    (
+        g_fine, g_down, g_up, l_down, l_bottom, l_mid, l_fine,
+        w_menc, w_bot, w_q, w_k, w_v, w_o, w_umid, w_mdec, w_ufine, w_hd,
+    ) = near
     mx, mv = nx // 2, nv // 2
     bx, bv = nx // 4, nv // 4
     ix, iy, iz = lax.axis_index("gx"), lax.axis_index("gy"), lax.axis_index("gz")
@@ -199,6 +211,8 @@
         for c in range(3):
             t_first[(c * (nv + 2) + k) * 16 : (c * (nv + 2) + k + 1) * 16] = part[c * 16 : c * 16 + 16]
     across = finish(0, made, p_in, q_in)
+    for c in fetches:
+        c.wait()
     for src, dst in ((w_enc, t_enc), (w_dec, t_dec)):
         flat = by_tap(src)
         for k in range(nv):
@@ -401,10 +415,14 @@
     w_umid = w_up_mid.reshape(2, 2, 2, 256, 64).transpose(0, 1, 4, 2, 3).reshape(256, 512)
     w_ufine = w_up_fine.transpose(2, 3, 1, 4, 0).reshape(64, 128)
     w_hd = (w_head[:, None, None, :] * jnp.eye(nv, dtype=BF)[None, :, :, None]).reshape(4 * nv, nv * 16)
+    g_first, *fixed = constants(nx, nv, ns)
+    far = (
+        *fixed, mid(w_mid_enc), w_bot, w_query, w_key, w_value, w_attn_out, w_umid, mid(w_mid_dec), w_ufine, w_hd,
+    )
+    assert len(far) == FAR
     operands = (
-        local, each_tap(w_in), each_tap(w_fine_enc), taps_out(w_down_mid), mid(w_mid_enc), w_bot,
-        w_query, w_key, w_value, w_attn_out, w_umid, mid(w_mid_dec), w_ufine, each_tap(w_fine_dec), w_hd,
-    ) + constants(nx, nv, ns)
+        local, each_tap(w_in), each_tap(w_fine_enc), taps_out(w_down_mid), g_first, each_tap(w_fine_dec),
+    )
     vm = pltpu.VMEM
     shapes = []
     for shape in (
@@ -415,7 +433,8 @@
     return pl.pallas_call(
         functools.partial(kernel, gx, gz, nx, nv, ns),
         out_shape=jax.ShapeDtypeStruct(inputs.shape, F32),
-        in_specs=[pl.BlockSpec(memory_space=pltpu.VMEM)] * len(operands),
+        in_specs=[pl.BlockSpec(memory_space=pltpu.VMEM)] * len(operands)
+        + [pl.BlockSpec(memory_space=pl.ANY)] * FAR,
         out_specs=pl.BlockSpec(memory_space=pltpu.VMEM),
         scratch_shapes=shapes + [
             vm((3 * (nv + 2) * 16, 3 * (nv + 8) * 4), BF),
@@ -435,11 +454,12 @@
             pltpu.SemaphoreType.DMA((4,)),
             pltpu.SemaphoreType.DMA((max(gx - 1, 1),)),
             pltpu.SemaphoreType.DMA((max(gx - 1, 1),)),
-        ],
+            pltpu.SemaphoreType.DMA((FAR,)),
+        ] + [vm(a.shape, BF) for a in far],
         compiler_params=pltpu.CompilerParams(
             collective_id=0, has_side_effects=True, vmem_limit_bytes=48 * 1024 * 1024
         ),
-    )(*operands)
+    )(*operands, *far)
 
 
 def solution(mesh):

time: 85.7 us -> 88 us (1.027)
  Pallas kernels: 63.5 us -> 65.7 us
    pallas_call x1, Pallas kernels: 63.5 us -> 65.7 us  [on_device(): pl.pallas_call(functools.partial(kernel, gx, gz, nx, nv, ns), out_shape=j...]
where the time goes in v2:
time: 88 us; the launch traced here: 87.4 us
  Pallas kernels  65.7 us (75%)
  local copies, waits for them, and re-layouts  21.4 us (24%)
    pallas_call x1, Pallas kernels, on_device(): pl.pallas_call(functools.partial(kernel, gx, gz, nx, nv, ns), out_shape=j...  65.7 us
    unnamed x42, local copies, waits for them, and re-layouts  8.9 us
    reshape x6, local copies, waits for them, and re-layouts, mid(): return w.reshape(3, 3, 3, 64, 64).transpose(2, 3, 0, 1, 4).reshape(192, 576)  3.45 us
    reshape x2, local copies, waits for them, and re-layouts, on_device(): w_down_bottom.reshape(2, 2, 2, 256, 64).transpose(3, 2, 0, 1, 4)  2.43 us
    transpose x1, local copies, waits for them, and re-layouts, on_device(): w_down_bottom.reshape(2, 2, 2, 256, 64).transpose(3, 2, 0, 1, 4)  2.07 us

profile of v2, /device:TPU:3, one launch (start us, length us, event | category | flops | bytes accessed | tf_op | source)
XLA Modules:
  0.0 87.4 jit_solution(8581808279855733579)
XLA Ops:
  0.0 1.5 %reshape.60 = bf16[3,3,3,64,64]{4,3,2,1,0:T(8,128)(2,1)S(1)} reshape(bf16[27,4096]{1,0:T(8,128)(2,1)} %param.27) | data formatting | bytes 442368 | tf_op jit(solution)/shard_map/reshape | solution.py:411
  1.5 0.4 copy.46
  1.9 0.4 reshape.61.rest_7_
  2.3 0.4 reshape.66
  2.7 0.4 copy.45
  3.1 0.4 reshape.67.rest_14_
  3.5 0.5 reshape.64
  4.1 0.2 copy.37
  4.4 0.1 copy-done.15
  4.5 1.3 %reshape.62 = bf16[2,2,2,256,64]{4,3,2,1,0:T(8,128)(2,1)} reshape(bf16[8,16384]{1,0:T(8,128)(2,1)S(1)} %copy-done.15) | data formatting | bytes 524288 | tf_op jit(solution)/shard_map/reshape | solution.py:414
  5.8 2.1 %copy.36 = bf16[256,2,2,2,64]{0,4,3,2,1:T(8,128)(2,1)} copy(bf16[256,2,2,2,64]{4,0,1,3,2:T(8,128)(2,1)} %bitcast.36) | data formatting | bytes 524288 | tf_op jit(solution)/shard_map/transpose | solution.py:414
  7.9 1.1 %copy.41.rest_8_ = bf16[256,512]{1,0:T(8,128)(2,1)S(1)} copy(bf16[256,512]{0,1:T(8,128)(2,1)} %bitcast.38) | data formatting | bytes 524288 | tf_op jit(solution)/shard_map/reshape | solution.py:414
  9.0 0.3 copy.33
  9.3 0.1 reshape.58
  9.4 0.1 copy.40.w_down
  9.5 0.1 broadcast_multiply_fusion
  9.6 0.1 mul.20.rest_16_
  9.7 0.9 %copy.32 = bf16[8,8,4,128]{3,2,1,0:T(4,128)(2,1)S(1)} copy(bf16[8,8,4,128]{3,1,0,2:T(8,128)(2,1)} %bitcast.39) | data formatting | bytes 131072 | tf_op jit(solution)/shard_map/transpose | solution.py:413
  10.6 1.4 %copy.39 = bf16[2,2,16,2,64]{4,3,2,1,0:T(2,128)(2,1)} copy(bf16[2,2,16,2,64]{4,3,1,0,2:T(2,128)(2,1)} %bitcast.41) | data formatting | bytes 32768 | tf_op jit(solution)/shard_map/transpose | solution.py:416
  12.0 0.8 reshape.68.rest_15_
  12.9 0.0 copy-start.4
  12.9 0.9 %copy-done.4 = bf16[10,36,192]{2,1,0:T(8,128)(2,1)S(1)} copy-done((bf16[10,36,192]{2,1,0:T(8,128)(2,1)S(1)}, bf16[10,36,192]{2,1,0:T(8,128)(2,1)}, u32[]{:S(2)}) %copy-start.4) | copy-done | bytes 138264
  13.9 0.9 %copy-done.5 = bf16[256,256]{1,0:T(8,128)(2,1)S(1)} copy-done((bf16[256,256]{1,0:T(8,128)(2,1)S(1)}, bf16[256,256]{1,0:T(8,128)(2,1)}, u32[]{:S(2)}) %copy-start.5) | copy-done | bytes 131096
  14.8 0.9 %copy-done.6 = bf16[256,256]{1,0:T(8,128)(2,1)S(1)} copy-done((bf16[256,256]{1,0:T(8,128)(2,1)S(1)}, bf16[256,256]{1,0:T(8,128)(2,1)}, u32[]{:S(2)}) %copy-start.6) | copy-done | bytes 131096
  15.7 0.9 %copy-done.7 = bf16[256,256]{1,0:T(8,128)(2,1)S(1)} copy-done((bf16[256,256]{1,0:T(8,128)(2,1)S(1)}, bf16[256,256]{1,0:T(8,128)(2,1)}, u32[]{:S(2)}) %copy-start.7) | copy-done | bytes 131096
  16.6 0.9 %copy-done.8 = bf16[256,256]{1,0:T(8,128)(2,1)S(1)} copy-done((bf16[256,256]{1,0:T(8,128)(2,1)S(1)}, bf16[256,256]{1,0:T(8,128)(2,1)}, u32[]{:S(2)}) %copy-start.8) | copy-done | bytes 131096
  17.5 0.9 %copy-done.9 = bf16[4,64,256]{2,1,0:T(8,128)(2,1)S(1)} copy-done((bf16[4,64,256]{2,1,0:T(8,128)(2,1)S(1)}, bf16[4,64,256]{2,1,0:T(8,128)(2,1)}, u32[]{:S(2)}) %copy-start.9) | copy-done | bytes 131096
  18.4 0.9 %copy-done.10 = bf16[16,16,3,3,3]{1,0,4,3,2:T(8,128)(2,1)S(1)} copy-done((bf16[16,16,3,3,3]{1,0,4,3,2:T(8,128)(2,1)S(1)}, bf16[16,16,3,3,3]{1,0,4,3,2:T(8,128)(2,1)}, u32[]{:S(2)}) %copy-start.10) | copy-done | bytes 13848
  19.3 0.9 %copy-done.11 = bf16[16,16,3,3,3]{1,0,4,3,2:T(8,128)(2,1)S(1)} copy-done((bf16[16,16,3,3,3]{1,0,4,3,2:T(8,128)(2,1)S(1)}, bf16[16,16,3,3,3]{1,0,4,3,2:T(8,128)(2,1)}, u32[]{:S(2)}) %copy-start.11) | copy-done | bytes 13848
  20.2 0.8 copy-done.13
  21.0 65.7 %shard_map.217 = f32[4,8,8,128]{3,2,1,0:T(8,128)S(1)} custom-call(bf16[8,32,128]{2,1,0:T(8,128)(2,1)S(1)} %bitcast.30, bf16[27,16,4]{2,1,0:T(8,128)(2,1)S(1)} %bitcast.29, bf16[27,16,16]{2,1,0:T(8,128)(2,1)S(1)} %bitcast.31, bf16[128,64]{1,0:T(8,128)(2,1)S(1)} %copy.40.w_down, bf16[10,36,192]{2,1,0:T(8,128)(2,1)S(1)} %copy-done.4, ...), custom_call_target="tpu_custom_call" | custom-call | tf_op jit(solution)/shard_map/pallas_call | solution.py:433
  86.7 0.7 copy.48
  (32 shorter events, 0.1 us)
Async XLA Ops:
  0.0 2.3 %copy-start.16 = (bf16[27,4096]{1,0:T(8,128)(2,1)S(1)}, bf16[27,4096]{1,0:T(8,128)(2,1)}, u32[]{:S(2)}) copy-start(bf16[27,4096]{1,0:T(8,128)(2,1)} %param.34) | copy-start | bytes 663556
  2.3 1.3 %copy-start.14 = (bf16[8,16384]{1,0:T(8,128)(2,1)S(1)}, bf16[8,16384]{1,0:T(8,128)(2,1)}, u32[]{:S(2)}) copy-start(bf16[8,16384]{1,0:T(8,128)(2,1)} %param.33) | copy-start | bytes 786436
  3.5 1.0 %copy-start.15 = (bf16[8,16384]{1,0:T(8,128)(2,1)S(1)}, bf16[8,16384]{1,0:T(8,128)(2,1)}, u32[]{:S(2)}) copy-start(bf16[8,16384]{1,0:T(8,128)(2,1)} %param.28) | copy-start | bytes 786436
  4.4 4.6 %copy-start.18 = (bf16[16,4,3,3,3]{0,1,4,3,2:T(4,128)(2,1)S(1)}, bf16[16,4,3,3,3]{0,1,4,3,2:T(4,128)(2,1)}, u32[]{:S(2)}) copy-start(bf16[16,4,3,3,3]{0,1,4,3,2:T(4,128)(2,1)} %param.24) | copy-start | bytes 10372
  4.4 4.9 %copy-start.17 = (bf16[64,16,2,2,2]{0,4,3,2,1:T(2,128)(2,1)S(1)}, bf16[64,16,2,2,2]{0,4,3,2,1:T(2,128)(2,1)}, u32[]{:S(2)}) copy-start(bf16[64,16,2,2,2]{0,4,3,2,1:T(2,128)(2,1)} %param.26) | copy-start | bytes 49156
  4.5 5.0 %copy-start.19 = (bf16[4,16]{1,0:T(4,128)(2,1)S(1)}, bf16[4,16]{1,0:T(4,128)(2,1)}, u32[]{:S(2)}) copy-start(bf16[4,16]{1,0:T(4,128)(2,1)} %param.37) | copy-start | bytes 388
  4.5 8.4 %copy-start.3 = (bf16[128,1024]{1,0:T(8,128)(2,1)S(1)}, bf16[128,1024]{1,0:T(8,128)(2,1)}, u32[]{:S(2)}) copy-start(bf16[128,1024]{1,0:T(8,128)(2,1)} %constant.22.clone.rest_5_) | copy-start | bytes 786436
  4.5 8.4 %copy-start.12 = (bf16[128,256]{1,0:T(8,128)(2,1)S(1)}, bf16[128,256]{1,0:T(8,128)(2,1)}, u32[]{:S(2)}) copy-start(bf16[128,256]{1,0:T(8,128)(2,1)} %constant.20.clone.rest_3_) | copy-start | bytes 196612
  5.8 7.1 %copy-start = (bf16[8,144,480]{2,1,0:T(8,128)(2,1)S(1)}, bf16[8,144,480]{2,1,0:T(8,128)(2,1)}, u32[]{:S(2)}) copy-start(bf16[8,144,480]{2,1,0:T(8,128)(2,1)} %constant.17.clone.rest_0_) | copy-start | bytes 3317764
  5.8 7.1 %copy-start.1 = (bf16[4,128,512]{2,1,0:T(8,128)(2,1)S(1)}, bf16[4,128,512]{2,1,0:T(8,128)(2,1)}, u32[]{:S(2)}) copy-start(bf16[4,128,512]{2,1,0:T(8,128)(2,1)} %constant.19.clone.rest_2_) | copy-start | bytes 1572868
  5.8 7.1 %copy-start.2 = (bf16[4,128,256]{2,1,0:T(8,128)(2,1)S(1)}, bf16[4,128,256]{2,1,0:T(8,128)(2,1)}, u32[]{:S(2)}) copy-start(bf16[4,128,256]{2,1,0:T(8,128)(2,1)} %constant.21.clone.rest_4_) | copy-start | bytes 786436
  12.9 0.9 %copy-start.4 = (bf16[10,36,192]{2,1,0:T(8,128)(2,1)S(1)}, bf16[10,36,192]{2,1,0:T(8,128)(2,1)}, u32[]{:S(2)}) copy-start(bf16[10,36,192]{2,1,0:T(8,128)(2,1)} %constant.16.clone.g_first) | copy-start | bytes 414724
  13.9 0.9 %copy-start.5 = (bf16[256,256]{1,0:T(8,128)(2,1)S(1)}, bf16[256,256]{1,0:T(8,128)(2,1)}, u32[]{:S(2)}) copy-start(bf16[256,256]{1,0:T(8,128)(2,1)} %rest_9_.1) | copy-start | bytes 393220
  14.8 0.9 %copy-start.6 = (bf16[256,256]{1,0:T(8,128)(2,1)S(1)}, bf16[256,256]{1,0:T(8,128)(2,1)}, u32[]{:S(2)}) copy-start(bf16[256,256]{1,0:T(8,128)(2,1)} %rest_10_.1) | copy-start | bytes 393220
  15.7 0.9 %copy-start.7 = (bf16[256,256]{1,0:T(8,128)(2,1)S(1)}, bf16[256,256]{1,0:T(8,128)(2,1)}, u32[]{:S(2)}) copy-start(bf16[256,256]{1,0:T(8,128)(2,1)} %rest_11_.1) | copy-start | bytes 393220
  16.6 0.9 %copy-start.8 = (bf16[256,256]{1,0:T(8,128)(2,1)S(1)}, bf16[256,256]{1,0:T(8,128)(2,1)}, u32[]{:S(2)}) copy-start(bf16[256,256]{1,0:T(8,128)(2,1)} %rest_12_.1) | copy-start | bytes 393220
  17.5 0.9 %copy-start.9 = (bf16[4,64,256]{2,1,0:T(8,128)(2,1)S(1)}, bf16[4,64,256]{2,1,0:T(8,128)(2,1)}, u32[]{:S(2)}) copy-start(bf16[4,64,256]{2,1,0:T(8,128)(2,1)} %constant.18.clone.rest_1_) | copy-start | bytes 393220
  18.4 0.9 %copy-start.10 = (bf16[16,16,3,3,3]{1,0,4,3,2:T(8,128)(2,1)S(1)}, bf16[16,16,3,3,3]{1,0,4,3,2:T(8,128)(2,1)}, u32[]{:S(2)}) copy-start(bf16[16,16,3,3,3]{1,0,4,3,2:T(8,128)(2,1)} %param.25) | copy-start | bytes 41476
  19.3 0.9 %copy-start.11 = (bf16[16,16,3,3,3]{1,0,4,3,2:T(8,128)(2,1)S(1)}, bf16[16,16,3,3,3]{1,0,4,3,2:T(8,128)(2,1)}, u32[]{:S(2)}) copy-start(bf16[16,16,3,3,3]{1,0,4,3,2:T(8,128)(2,1)} %param.36) | copy-start | bytes 41476
  20.2 0.8 copy-start.13
